TPU v7x, 512 devices: a whole 4x4x16 slice. The times are simulated.
512 devices in a mesh: member: 8 (over y, core), dp: 4 (over x), block: 16 (over z).
Axes of the slice: x: 4, y: 4, z: 16, core: 2. Of those that a mesh axis runs over, the one named last changes fastest.
Arguments:
- a_train: bfloat16 [16384, 1024], P(('member', 'block'), 'dp'), parts along dimension 0, may hold values from -6 to 6
- g_train: bfloat16 [32768, 1024], P(('member', 'block'), 'dp'), parts along dimension 0, may hold values from -6 to 6
- a_query: bfloat16 [16384, 128], P(('member', 'block')), parts along dimension 0, may hold values from -6 to 6
- g_query: bfloat16 [32768, 128], P(('member', 'block')), parts along dimension 0, may hold values from -6 to 6
- basis_in: bfloat16 [16384, 2048], P('member', 'block'), parts along dimension 0, may hold values from -0.125 to 0.125
- basis_out: bfloat16 [32768, 4096], P('member', 'block'), parts along dimension 0, may hold values from -0.09375 to 0.09375
- eigen: float32 [16384, 4096], P(('member', 'block'), 'dp'), parts along dimension 0, may hold values from 0.05 to 5
Outputs:
- influence: float32 [64, 64], P('member', 'dp'), parts along dimension 0
There are 8 independent parts, one for each index of `member`. A program takes and returns all parts, laid end to end along the dimension named above; each array names one. Nothing has to cross between parts.
All inputs are finite; a program needn't handle non-finite values.
Results may differ from a plain program's by a relative error of at most 0.0052.
Values may be sent and summed in bfloat16 or wider, within the bound.
A program may use at most 64 MiB of HBM per device.

v0:
```python
import jax
import jax.numpy as jnp
from jax import lax
from jax.sharding import PartitionSpec as P

STEPS = 16
NQ = 8
QSTEPS = 16


damping = 0.05


def rotate_adder(basis, piece):
    return lax.dot_general(
        basis, piece, (((0,), (0,)), ((), ())), preferred_element_type=jnp.float32
    )


def score_terms(precond, rot_gt, train_af, n_queries, n_steps):
    inner = jnp.einsum("qij,jr->qir", precond, rot_gt, preferred_element_type=jnp.float32)
    column_score = jnp.sum(inner * train_af[None], axis=1)
    return column_score.reshape(n_queries, -1, n_steps).sum(axis=2)


def shards(a_train, g_train, a_query, g_query, basis_in, basis_out, eigen):
    train_cols = a_train.shape[1]
    width_in = a_train.shape[0]
    joined_a = jnp.concatenate([a_train, a_query], axis=1)
    joined_g = jnp.concatenate([g_train, g_query], axis=1)
    rot_a = rotate_adder(basis_in, lax.all_gather(joined_a, "block", axis=0, tiled=True)).astype(
        jnp.bfloat16
    )
    rot_g_local = rotate_adder(
        basis_out, lax.all_gather(joined_g, "block", axis=0, tiled=True)
    ).astype(jnp.bfloat16)
    rot_g = lax.all_gather(rot_g_local, "block", axis=0, tiled=True)
    rot_at = rot_a[:, :train_cols]
    rot_aq = rot_a[:, train_cols:]
    rot_gt = rot_g[:, :train_cols]
    rot_gq = rot_g[:, train_cols:]
    query_a = rot_aq.reshape(width_in, NQ, QSTEPS).transpose(1, 0, 2)
    train_af = rot_at.astype(jnp.float32)
    width_cols = eigen.shape[1]
    column_start = lax.axis_index("dp") * width_cols
    query_cols = lax.dynamic_slice_in_dim(rot_gq, column_start, width_cols, 0)
    query_g = query_cols.reshape(width_cols, NQ, QSTEPS).transpose(1, 0, 2)
    query_grad = jnp.einsum("qir,qjr->qij", query_a, query_g, preferred_element_type=jnp.float32)
    damped = eigen + damping
    precond_local = (query_grad / damped[None]).astype(jnp.bfloat16)
    norm_terms = jnp.sum(query_grad * query_grad / damped[None], axis=(1, 2))
    norm_value = lax.psum(norm_terms, ("dp", "block"))
    precond = lax.all_gather(precond_local, "dp", axis=2, tiled=True)
    partial_value = score_terms(precond, rot_gt, train_af, NQ, STEPS)
    scores = lax.psum(partial_value, "block")
    return scores / jnp.sqrt(norm_value * STEPS)[:, None]


def solution(mesh):
    in_specs = (
        P(("member", "block"), "dp"),
        P(("member", "block"), "dp"),
        P(("member", "block"), None),
        P(("member", "block"), None),
        P("member", "block"),
        P("member", "block"),
        P(("member", "block"), "dp"),
    )
    out_specs = P("member", "dp")
    return jax.shard_map(shards, mesh=mesh, in_specs=in_specs, out_specs=out_specs, check_vma=False)
```

profile of v0, /device:TPU:24, one launch (start us, length us, event | category | flops | bytes accessed | tf_op | source)
XLA Modules:
  0.0 434.6 jit_solution(13620236759793878511)
XLA Ops:
  6.5 1.8 pad_maximum_fusion
  8.3 0.0 all-gather.7.cloned.1.call-update
  8.4 0.0 all-gather.5.cloned.1.call-start
  8.4 1.5 pad_maximum_fusion.1
  9.9 0.0 all-gather.5.cloned.1.call-update
  9.9 0.0 all-gather.9.cloned.1.call-start
  10.0 79.8 %all-gather.7.cloned.1.call-done = bf16[4096,384]{1,0:T(8,128)(2,1)} async-done(((bf16[256,384]{1,0:T(8,128)(2,1)}), bf16[4096,384]{1,0:T(8,128)(2,1)}) %all-gather.7.cloned.1.call-update) | async-done | bytes 3145744 | tf_op jit(solution)/shard_map/all_gather | solution.py:35
  89.8 3.6 fusion.4
  93.4 0.0 all-gather.9.cloned.1.call-update
  93.4 0.0 all-gather.11.cloned.1.call-start
  93.5 0.1 broadcast_add_fusion
  93.6 67.7 %all-gather.5.cloned.1.call-done = bf16[2048,384]{1,0:T(8,128)(2,1)} async-done(((bf16[128,384]{1,0:T(8,128)(2,1)}), bf16[2048,384]{1,0:T(8,128)(2,1)}) %all-gather.5.cloned.1.call-update) | async-done | bytes 1572880 | tf_op jit(solution)/shard_map/all_gather | solution.py:31
  161.3 2.1 fusion.5
  163.4 84.1 %all-gather.9.cloned.1.call-done = bf16[4096,384]{0,1:T(8,128)(2,1)} async-done(((bf16[256,384]{0,1:T(8,128)(2,1)}), bf16[4096,384]{0,1:T(8,128)(2,1)}) %all-gather.9.cloned.1.call-update) | async-done | bytes 3145744 | tf_op jit(solution)/shard_map/all_gather | solution.py:37
  247.5 1.3 slice.17
  248.9 2.3 fusion
  251.2 0.0 all-gather.11.cloned.1.call-update
  251.2 0.1 copy.11
  251.4 142.4 %psum.15 = f32[8]{0:T(128)S(1)} all-reduce(f32[8]{0:T(128)S(1)} %get-tuple-element.5), channel_id=1, replica_groups=mesh['member'=8,'dp'=4,'block'=16] {'dp','block'}, use_global_device_ids=true, to_apply=%region_4.0 | all-reduce | flops 8 | bytes 64 | tf_op jit(solution)/shard_map/psum | solution.py:52
  393.8 6.4 %fusion.3 = f32[8,256]{1,0:T(8,128)S(1)} fusion(bf16[8,128,4096]{2,1,0:T(8,128)(2,1)} %all-gather.11.cloned.1.call-done, bf16[4096,384]{0,1:T(8,128)(2,1)} %all-gather.9.cloned.1.call-done, f32[128,256]{1,0:T(8,128)S(1)} %copy.11), kind=kOutput, calls=%fused_computation.6 | convolution fusion | flops 2148005888 | bytes 10625024 | tf_op jit(solution)/shard_map/qij,jr->qir/dot_general | solution.py:21
  400.2 0.1 reshape.14
  400.2 0.1 reduce_sum.28
  400.3 27.0 %psum.14 = f32[8,16]{1,0:T(8,128)S(1)} all-reduce(f32[8,16]{1,0:T(8,128)S(1)} %reduce_sum.28), channel_id=1, replica_groups=mesh['member'=8,'dp'=4,'block'=16] {'block'}, use_global_device_ids=true, to_apply=%region_2.0 | all-reduce | flops 128 | bytes 1024 | tf_op jit(solution)/shard_map/psum | solution.py:55
  427.4 0.7 broadcast_divide_fusion
  (10 shorter events, 0.1 us)
Async XLA Ops:
  6.5 83.3 %copy-start = (bf16[4096,256]{1,0:T(8,128)(2,1)S(1)}, bf16[4096,256]{1,0:T(8,128)(2,1)}, u32[]{:S(2)}) copy-start(bf16[4096,256]{1,0:T(8,128)(2,1)} %param.12) | copy-start | bytes 6291460
  6.5 83.3 %all-gather.7.cloned.1.call-start = ((), (), s32[]{:S(2)}) async-start(), calls=%async_computation.1 | async-start | bytes 3342336 | tf_op jit(solution)/shard_map/all_gather | solution.py:35
  8.4 152.9 %all-gather.5.cloned.1.call-start = ((), (), s32[]{:S(2)}) async-start(), calls=%async_computation | async-start | bytes 1671168 | tf_op jit(solution)/shard_map/all_gather | solution.py:31
  9.9 83.6 %copy-start.1 = (f32[128,1024]{1,0:T(8,128)S(1)}, f32[128,1024]{1,0:T(8,128)}, u32[]{:S(2)}) copy-start(f32[128,1024]{1,0:T(8,128)} %param.13) | copy-start | bytes 1572868
  9.9 237.6 %all-gather.9.cloned.1.call-start = ((), (), s32[]{:S(2)}) async-start(), calls=%async_computation.2 | async-start | bytes 3342336 | tf_op jit(solution)/shard_map/all_gather | solution.py:37
  93.4 300.3 %all-gather.11.cloned.1.call-start = ((), (), s32[]{:S(2)}) async-start(), calls=%async_computation.3 | async-start | bytes 10485760 | tf_op jit(solution)/shard_map/all_gather | solution.py:53
Sparse Core Ops, SparseCore 0:
  9.4 80.3 all-gather.6
  91.9 69.3 all-gather.4
  163.3 84.1 all-gather.8
  251.4 87.5 all-gather.10
where the time goes:
time: 435 us
  waiting for transfers between devices  232 us (53%)
  blocking collectives  169 us (39%)
  matrix products  14.4 us (3%)
  between operations  13.2 us (3%)
    psum x1, blocking collectives, shards(): norm_value = lax.psum(norm_terms, ('dp', 'block'))  142 us
    all_gather x1, waiting for transfers between devices, shards(): rot_g = lax.all_gather(rot_g_local, 'block', axis=0, tiled=True)  84.1 us
    all_gather x1, waiting for transfers between devices, shards(): lax.all_gather(joined_g, 'block', axis=0, tiled=True)  79.8 us
    all_gather x1, waiting for transfers between devices, shards(): lax.all_gather(joined_a, 'block', axis=0, tiled=True)  67.7 us
    psum x1, blocking collectives, shards(): scores = lax.psum(partial_value, 'block')  27 us
  transfers between devices with their start and end apart: 4, of which 3 were waited for; matrix products, arithmetic and copies ran while one was open for 2% of the time, Pallas kernels for 0%

commit v1 on v0

v1 whole, which is shorter than its diff:
```python
import functools

import jax
import jax.numpy as jnp
from jax import lax
from jax.experimental import pallas as pl
from jax.experimental.pallas import tpu as pltpu
from jax.sharding import PartitionSpec as P

STEPS = 16
NQ = 8
QSTEPS = 16
DAMPING = 0.05

MESH = pl.DeviceIdType.MESH
BF16 = jnp.bfloat16
F32 = jnp.float32


def contract_rows(left, right):
    return lax.dot_general(left, right, (((0,), (0,)), ((), ())), preferred_element_type=F32)


def kernel(
    nz, nx,
    a_ref, g_ref, aq_ref, gq_ref, bi_ref, bo_ref, eig_ref,
    out_ref,
    g_buf, a_buf, gq_buf, aq_buf, rg_buf, rgq_buf, bo, bi, eig, inv,
    g_acc, a_acc, gq_part, gq_recv, aq_part, aq_recv, aq_mask, x_acc, norm_acc, msg, sums,
    ring_send, ring_recv, x_send, x_recv, xg_send, xg_recv, z_send, z_recv, local_sem,
):
    half = nz // 2
    me = lax.axis_index("block")
    dp = lax.axis_index("dp")
    n_in, n_t = a_ref.shape
    n_out = g_ref.shape[0]
    n_c = aq_ref.shape[1]
    q_in, q_out = n_in // nx, n_out // nx
    per_dp = nz // nx

    def z_peer(k):
        return {"block": lax.rem(me + (k + nz), nz)}

    def x_peer(k):
        return {"dp": lax.rem(dp + k, nx)}

    def source(slot):
        return lax.rem(me + nz - slot, nz)

    locals_ = [
        pltpu.make_async_copy(eig_ref, eig, local_sem.at[0]),
        pltpu.make_async_copy(bo_ref, bo, local_sem.at[1]),
        pltpu.make_async_copy(g_ref, g_buf.at[0], local_sem.at[2]),
        pltpu.make_async_copy(bi_ref, bi, local_sem.at[3]),
        pltpu.make_async_copy(a_ref, a_buf.at[0], local_sem.at[4]),
        pltpu.make_async_copy(gq_ref.at[pl.ds(pl.multiple_of(dp * q_out, q_out), q_out)], gq_buf.at[0], local_sem.at[5]),
        pltpu.make_async_copy(aq_ref.at[pl.ds(pl.multiple_of(dp * q_in, q_in), q_in)], aq_buf.at[0], local_sem.at[6]),
    ]
    for copy in locals_:
        copy.start()

    barrier = pltpu.get_barrier_semaphore()
    for k in range(1, nz):
        pl.semaphore_signal(barrier, inc=1, device_id=z_peer(k), device_id_type=MESH)
    for k in range(1, nx):
        pl.semaphore_signal(barrier, inc=1, device_id=x_peer(k), device_id_type=MESH)

    def ring(index, buf, first, rows):
        start, size = rows
        start = start if isinstance(start, int) else pl.multiple_of(start, size)

        def at(ref, lo, n):
            return ref.at[pl.ds(start + lo, n)]

        def copy(way, hop, part):
            lo, n = (0, size) if not part else ((0, size // 2) if way == 0 else (size // 2, size // 2))
            own = isinstance(hop, int) and hop == 0
            src_slot, dst_slot = (hop, hop + 1) if way == 0 else (lax.rem(nz - hop, nz), nz - 1 - hop)
            src = at(first, lo, n) if own else at(buf.at[src_slot], lo, n)
            return pltpu.make_async_remote_copy(
                src_ref=src, dst_ref=at(buf.at[dst_slot], lo, n),
                send_sem=ring_send.at[index, way, hop], recv_sem=ring_recv.at[index, way, hop],
                device_id=z_peer(1 if way == 0 else -1), device_id_type=MESH,
            )

        def begin():
            for way in (0, 1):
                copy(way, 0, False).start()

        def step(hop):
            last = isinstance(hop, int) and hop == half
            for way in (0, 1):
                copy(way, hop - 1, last).wait_recv()
                if not last:
                    copy(way, hop, isinstance(hop, int) and hop == half - 1).start()

        def finish():
            for way in (0, 1):
                def body(hop, c):
                    copy(way, hop, False).wait_send()
                    return c
                copy(way, 0, False).wait_send()
                lax.fori_loop(1, half - 1, body, 0)
                copy(way, half - 1, True).wait_send()

        return begin, step, finish

    ho, hi = n_out // 2, n_in // 2
    gq_ring = ring(0, gq_buf, gq_buf.at[0], (0, q_out))
    g0_ring = ring(1, g_buf, g_ref, (0, ho))
    g1_ring = ring(2, g_buf, g_ref, (ho, ho))
    aq_ring = ring(3, aq_buf, aq_buf.at[0], (0, q_in))
    a0_ring = ring(4, a_buf, a_ref, (0, hi))
    a1_ring = ring(5, a_buf, a_ref, (hi, hi))
    rg0_ring = ring(6, rg_buf, rg_buf.at[0], (0, ho))
    rg1_ring = ring(7, rg_buf, rg_buf.at[0], (ho, ho))
    rgq_ring = ring(8, rgq_buf, rgq_buf.at[0], (dp * q_out, q_out))

    locals_[5].wait()
    locals_[6].wait()
    pl.semaphore_wait(barrier, nz - 1 + nx - 1)

    for one in (gq_ring, g0_ring, g1_ring, aq_ring, a0_ring):
        one[0]()

    locals_[0].wait()
    for k in range(per_dp):
        inv[dp * per_dp + k] = 1.0 / (eig[:, k * n_out:(k + 1) * n_out] + DAMPING)

    def inv_copy(k):
        mine = inv.at[pl.ds(dp * per_dp, per_dp)]
        return pltpu.make_async_remote_copy(
            src_ref=mine, dst_ref=mine, send_sem=x_send.at[0, k - 1], recv_sem=x_recv.at[0, k - 1],
            device_id=x_peer(k), device_id_type=MESH,
        )

    def inv_arrival(k):
        theirs = inv.at[pl.ds(lax.rem(dp + nx - k, nx) * per_dp, per_dp)]
        return pltpu.make_async_remote_copy(
            src_ref=theirs, dst_ref=theirs, send_sem=x_send.at[0, k - 1], recv_sem=x_recv.at[0, k - 1],
            device_id=x_peer(k), device_id_type=MESH,
        )

    for k in range(1, nx):
        inv_copy(k).start()

    def rotate_g(slot):
        rows = pl.ds(pl.multiple_of(source(slot) * n_out, n_out), n_out)
        return contract_rows(bo[rows, :], g_buf[slot])

    def rotate_a(slot):
        rows = pl.ds(pl.multiple_of(source(slot) * n_in, n_in), n_in)
        return contract_rows(bi[rows, :], a_buf[slot])

    for k in (1, 2, 3, 4):
        locals_[k].wait()
    g_acc[...] = rotate_g(0)
    x_acc[...] = jnp.zeros_like(x_acc)
    norm_acc[...] = jnp.zeros_like(norm_acc)

    def first(hop):
        gq_ring[1](hop)
        g0_ring[1](hop)
        g1_ring[1](hop)
        aq_ring[1](hop)

    def first_body(hop, c):
        first(hop)
        a0_ring[1](hop)
        g_acc[...] += rotate_g(hop) + rotate_g(nz - hop)
        return c

    lax.fori_loop(1, half - 1, first_body, 0)
    first(half - 1)
    a0_ring[1](half - 1)
    a1_ring[0]()
    g_acc[...] += rotate_g(half - 1) + rotate_g(half + 1)
    g0_ring[1](half)
    g1_ring[1](half)
    rg_buf[0] = (g_acc[...] + rotate_g(half)).astype(BF16)
    rg0_ring[0]()
    rg1_ring[0]()

    gq_ring[1](half)

    def stack(ref, width, n):
        pieces = []
        for slot in range(nz):
            at = pl.multiple_of(source(slot) * width + dp * n, n)
            pieces.append(ref[pl.ds(at, n), :])
        return jnp.concatenate(pieces, axis=0)

    gq_part[...] = contract_rows(stack(bo, n_out, q_out), gq_buf[...].reshape(nz * q_out, n_c))

    def gq_copy(k):
        rows = pl.ds(pl.multiple_of(lax.rem(dp + k, nx) * q_out, q_out), q_out)
        return pltpu.make_async_remote_copy(
            src_ref=gq_part.at[rows], dst_ref=gq_recv.at[k - 1],
            send_sem=x_send.at[1, k - 1], recv_sem=x_recv.at[1, k - 1], device_id=x_peer(k), device_id_type=MESH,
        )

    def aq_copy(k):
        return pltpu.make_async_remote_copy(
            src_ref=aq_part, dst_ref=aq_recv.at[k - 1],
            send_sem=x_send.at[2, k - 1], recv_sem=x_recv.at[2, k - 1], device_id=x_peer(k), device_id_type=MESH,
        )

    for k in range(1, nx):
        gq_copy(k).start()
    aq_ring[1](half)
    aq_part[...] = contract_rows(stack(bi, n_in, q_in), aq_buf[...].reshape(nz * q_in, n_c))
    for k in range(1, nx):
        aq_copy(k).start()
    a0_ring[1](half)
    a_acc[...] = rotate_a(0)

    my_rows = pl.ds(pl.multiple_of(dp * q_out, q_out), q_out)

    def rgq_copy(slot, k):
        mine = rgq_buf.at[slot, my_rows]
        return pltpu.make_async_remote_copy(
            src_ref=mine, dst_ref=mine, send_sem=xg_send.at[slot, k - 1], recv_sem=xg_recv.at[slot, k - 1],
            device_id=x_peer(k), device_id_type=MESH,
        )

    def rgq_arrival(slot, k):
        rows = pl.ds(pl.multiple_of(lax.rem(dp + nx - k, nx) * q_out, q_out), q_out)
        theirs = rgq_buf.at[slot, rows]
        return pltpu.make_async_remote_copy(
            src_ref=theirs, dst_ref=theirs, send_sem=xg_send.at[slot, k - 1], recv_sem=xg_recv.at[slot, k - 1],
            device_id=x_peer(k), device_id_type=MESH,
        )

    for k in range(1, nx):
        gq_copy(k).wait_recv()
    rgq_buf[0, my_rows] = (gq_part[my_rows] + gq_recv[0] + gq_recv[1] + gq_recv[2]).astype(BF16)
    rgq_ring[0]()
    for k in range(1, nx):
        rgq_copy(0, k).start()
    for k in range(1, nx):
        aq_copy(k).wait_recv()
    rot_aq = (aq_part[...] + aq_recv[0] + aq_recv[1] + aq_recv[2]).astype(BF16)
    column = lax.broadcasted_iota(jnp.int32, (n_in, n_c), 1)
    for q in range(NQ):
        aq_mask[q * n_in:(q + 1) * n_in, :] = jnp.where(column // QSTEPS == q, rot_aq.astype(F32), 0.0).astype(BF16)
    for k in range(1, nx):
        inv_arrival(k).wait_recv()

    group = 2

    def score_block(slot):
        block_inv = inv[source(slot)]
        queries = rgq_buf[slot]
        train = rg_buf[slot]
        for part in range(NQ // group):
            rows = pl.ds(part * group * n_in, group * n_in)
            grad = lax.dot_general(
                aq_mask[rows, :], queries, (((1,), (1,)), ((), ())), preferred_element_type=F32
            ).reshape(group, n_in, n_out)
            precond = grad * block_inv[None]
            terms = (grad * precond).reshape(group, n_in // 8, 8, n_out).sum(axis=1)
            for lane in range(n_out // 128):
                norm_acc[part * group:(part + 1) * group] += terms[:, :, lane * 128:(lane + 1) * 128]
            x_acc[rows, :] += jnp.dot(
                precond.astype(BF16).reshape(group * n_in, n_out), train, preferred_element_type=F32
            )

    def gather_sends(slot):
        for k in range(1, nx):
            rgq_copy(slot, k).start()

    def gather_waits(slot):
        for k in range(1, nx):
            rgq_arrival(slot, k).wait_recv()

    def second(hop):
        rg0_ring[1](hop)
        rg1_ring[1](hop)
        a1_ring[1](hop)

    second(1)
    a_acc[...] += rotate_a(1) + rotate_a(nz - 1)
    gather_waits(0)
    score_block(0)

    second(2)
    rgq_ring[1](1)
    gather_sends(1)
    gather_sends(nz - 1)
    a_acc[...] += rotate_a(2) + rotate_a(nz - 2)

    def second_body(hop, c):
        second(hop)
        rgq_ring[1](hop - 1)
        gather_sends(hop - 1)
        gather_sends(nz - hop + 1)
        a_acc[...] += rotate_a(hop) + rotate_a(nz - hop)
        gather_waits(hop - 2)
        score_block(hop - 2)
        gather_waits(nz - hop + 2)
        score_block(nz - hop + 2)
        return c

    lax.fori_loop(3, half - 1, second_body, 0)
    second(half - 1)
    rgq_ring[1](half - 2)
    gather_sends(half - 2)
    gather_sends(half + 2)
    a_acc[...] += rotate_a(half - 1) + rotate_a(half + 1)

    def late_body(slot, c):
        gather_waits(slot)
        score_block(slot)
        return c

    for slot in (half - 3, half + 3):
        late_body(slot, 0)
    rgq_ring[1](half - 1)
    gather_sends(half - 1)
    gather_sends(half + 1)
    for slot in (half - 2, half + 2):
        late_body(slot, 0)
    rgq_ring[1](half)
    gather_sends(half)
    second(half)
    a_acc[...] += rotate_a(half)
    lax.fori_loop(half - 1, half + 2, late_body, 0)

    rot_a = a_acc[...].astype(BF16).astype(F32)
    for q in range(NQ):
        msg_row = jnp.sum(x_acc[q * n_in:(q + 1) * n_in, :] * rot_a, axis=0, keepdims=True)
        g_acc[q:q + 1, :] = msg_row
    step_of = lax.broadcasted_iota(jnp.int32, (n_t, 128), 0) // STEPS
    episode = lax.broadcasted_iota(jnp.int32, (n_t, 128), 1)
    pick = jnp.where(step_of == episode, 1.0, 0.0)
    scores = jnp.dot(
        g_acc[0:NQ, :], pick, preferred_element_type=F32, precision=lax.Precision.HIGHEST
    )
    norms = jnp.sum(jnp.sum(norm_acc[...], axis=1), axis=1, keepdims=True)
    lanes = lax.broadcasted_iota(jnp.int32, (NQ, 128), 1)
    msg[...] = jnp.where(lanes == 127, norms, scores)

    def sum_copy(k):
        return pltpu.make_async_remote_copy(
            src_ref=msg, dst_ref=sums.at[k - 1], send_sem=z_send.at[k - 1], recv_sem=z_recv.at[k - 1],
            device_id=z_peer(k), device_id_type=MESH,
        )

    for k in range(1, nz):
        sum_copy(k).start()

    for one in (gq_ring, g0_ring, g1_ring, aq_ring, a0_ring, a1_ring, rg0_ring, rg1_ring, rgq_ring):
        one[2]()
    for k in range(1, nx):
        inv_copy(k).wait_send()
        gq_copy(k).wait_send()
        aq_copy(k).wait_send()

    def sent_body(slot, c):
        for k in range(1, nx):
            rgq_copy(slot, k).wait_send()
        return c

    lax.fori_loop(0, nz, sent_body, 0)
    total = msg[...]
    for k in range(1, nz):
        sum_copy(k).wait_recv()
        total += sums[k - 1]
    for k in range(1, nz):
        sum_copy(k).wait_send()
    out_ref[...] = total


def shards(nz, nx, a_train, g_train, a_query, g_query, basis_in, basis_out, eigen):
    n_in, n_t = a_train.shape
    n_out = g_train.shape[0]
    n_c = a_query.shape[1]
    q_in, q_out = n_in // nx, n_out // nx
    vmem = pltpu.VMEM
    dma = pltpu.SemaphoreType.DMA
    total = pl.pallas_call(
        functools.partial(kernel, nz, nx),
        out_shape=jax.ShapeDtypeStruct((NQ, 128), F32),
        in_specs=[pl.BlockSpec(memory_space=pl.ANY)] * 7,
        out_specs=pl.BlockSpec(memory_space=vmem),
        scratch_shapes=[
            vmem((nz, n_out, n_t), BF16),
            vmem((nz, n_in, n_t), BF16),
            vmem((nz, q_out, n_c), BF16),
            vmem((nz, q_in, n_c), BF16),
            vmem((nz, n_out, n_t), BF16),
            vmem((nz, n_out, n_c), BF16),
            vmem(basis_out.shape, BF16),
            vmem(basis_in.shape, BF16),
            vmem(eigen.shape, F32),
            vmem((nz, n_in, n_out), F32),
            vmem((n_out, n_t), F32),
            vmem((n_in, n_t), F32),
            vmem((n_out, n_c), F32),
            vmem((nx - 1, q_out, n_c), F32),
            vmem((n_in, n_c), F32),
            vmem((nx - 1, n_in, n_c), F32),
            vmem((NQ * n_in, n_c), BF16),
            vmem((NQ * n_in, n_t), F32),
            vmem((NQ, 8, 128), F32),
            vmem((NQ, 128), F32),
            vmem((nz - 1, NQ, 128), F32),
            dma((9, 2, nz // 2)),
            dma((9, 2, nz // 2)),
            dma((3, nx - 1)),
            dma((3, nx - 1)),
            dma((nz, nx - 1)),
            dma((nz, nx - 1)),
            dma((nz - 1,)),
            dma((nz - 1,)),
            dma((7,)),
        ],
        compiler_params=pltpu.CompilerParams(
            collective_id=0, has_side_effects=True, vmem_limit_bytes=48 * 2**20
        ),
    )(a_train, g_train, a_query, g_query, basis_in, basis_out, eigen)
    return total[:, : n_t // STEPS] / jnp.sqrt(total[:, 127:128] * STEPS)


def solution(mesh):
    in_specs = (
        P(("member", "block"), "dp"),
        P(("member", "block"), "dp"),
        P(("member", "block"), None),
        P(("member", "block"), None),
        P("member", "block"),
        P("member", "block"),
        P(("member", "block"), "dp"),
    )
    body = functools.partial(shards, mesh.shape["block"], mesh.shape["dp"])
    return jax.shard_map(body, mesh=mesh, in_specs=in_specs, out_specs=P("member", "dp"), check_vma=False)
```

time: 435 us -> 112 us (0.26)
  waiting for transfers between devices: 232 us -> 0 us
  blocking collectives: 169 us -> 0 us
  Pallas kernels: 0 us -> 104 us
  matrix products: 14.4 us -> 0 us
  between operations: 13.2 us -> 0.02 us
  local copies, waits for them, and re-layouts: 1.5 us -> 7.01 us
    all_gather x4 -> x0, waiting for transfers between devices: 232 us -> none  [the longest x1 84.1 us: shards(): rot_g = lax.all_gather(rot_g_local, 'block', axis=0, tiled=True)]
    psum x2 -> x0, blocking collectives: 169 us -> none  [the longest x1 142 us: shards(): norm_value = lax.psum(norm_terms, ('dp', 'block'))]
    pallas_call x0 -> x1, Pallas kernels: none -> 104 us  [shards(): pl.pallas_call(functools.partial(kernel, nz, nx), out_shape=jax.ShapeDtyp...]
    dot_general x4 -> x0, matrix products: 14.4 us -> none  [the longest x1 6.36 us: score_terms(): jnp.einsum('qij,jr->qir', precond, rot_gt, preferred_element_type=jnp.flo...]
    unnamed x4 -> x14, local copies, waits for them, and re-layouts: 0.01 us -> 7.01 us
  transfers between devices with their start and end apart: 4 -> 0, of which waited for: 3 -> 0; matrix products, arithmetic and copies ran while one was open for 2% -> 0% of each run, Pallas kernels for 0% -> 0%
where the time goes in v1:
time: 112 us; the launch traced here: 111 us
  Pallas kernels  104 us (93%)
  local copies, waits for them, and re-layouts  7.01 us (6%)
    pallas_call x1, Pallas kernels, shards(): pl.pallas_call(functools.partial(kernel, nz, nx), out_shape=jax.ShapeDtyp...  104 us
    unnamed x14, local copies, waits for them, and re-layouts  7.01 us

profile of v1, /device:TPU:24, one launch (start us, length us, event | category | flops | bytes accessed | tf_op | source)
XLA Modules:
  0.0 111.5 jit_solution(17359080917883764133)
XLA Ops:
  0.0 0.0 copy-start
  0.0 1.6 %copy-done = bf16[4096,256]{1,0:T(8,128)(2,1)S(1)} copy-done((bf16[4096,256]{1,0:T(8,128)(2,1)S(1)}, bf16[4096,256]{1,0:T(8,128)(2,1)}, u32[]{:S(2)}) %copy-start) | copy-done | bytes 2097176
  1.6 0.0 copy-start.1
  1.6 1.0 copy-done.1
  2.6 0.0 copy-start.2
  2.6 1.0 copy-done.2
  3.7 0.0 copy-start.3
  3.7 0.9 copy-done.3
  4.6 0.0 copy-start.4
  4.6 0.8 copy-done.4
  5.4 0.0 copy-start.5
  5.4 0.8 copy-done.5
  6.3 0.0 copy-start.6
  6.3 0.8 copy-done.6
  7.0 103.6 %shard_map.73 = f32[8,128]{1,0:T(8,128)S(1)} custom-call(bf16[128,256]{1,0:T(8,128)(2,1)S(1)} %copy-done.4, bf16[256,256]{1,0:T(8,128)(2,1)S(1)} %copy-done.3, bf16[128,128]{1,0:T(8,128)(2,1)S(1)} %copy-done.6, bf16[256,128]{1,0:T(8,128)(2,1)S(1)} %copy-done.5, bf16[2048,128]{1,0:T(8,128)(2,1)S(1)} %copy-done.1, bf16[4096,256]{1,0:T(8,128)(2,1)S(1)} %copy-done, ...), custom_call_target="tpu_custom_call" | custom-call | tf_op jit(solution)/shard_map/pallas_call | solution.py:381
  110.6 0.2 sqrt_reduce_fusion
  110.8 0.7 slice_divide_fusion
Async XLA Ops:
  0.0 1.6 %copy-start = (bf16[4096,256]{1,0:T(8,128)(2,1)S(1)}, bf16[4096,256]{1,0:T(8,128)(2,1)}, u32[]{:S(2)}) copy-start(bf16[4096,256]{1,0:T(8,128)(2,1)} %bo_ref.1) | copy-start | bytes 6291460
  1.6 1.0 copy-start.1
  2.6 1.0 copy-start.2
  3.7 0.9 copy-start.3
  4.6 0.8 copy-start.4
  5.4 0.8 copy-start.5
  6.3 0.8 copy-start.6

commit v2 on v0

v2 whole, which is shorter than its diff:
```python
import functools

import jax
import jax.numpy as jnp
from jax import lax
from jax.experimental import pallas as pl
from jax.experimental.pallas import tpu as pltpu
from jax.sharding import PartitionSpec as P

STEPS = 16
NQ = 8
QSTEPS = 16
DAMPING = 0.05

MESH = pl.DeviceIdType.MESH
BF16 = jnp.bfloat16
F32 = jnp.float32


def contract_rows(left, right):
    return lax.dot_general(left, right, (((0,), (0,)), ((), ())), preferred_element_type=F32)


def kernel(
    nz, nx, a_lead,
    a_ref, g_ref, aq_ref, gq_ref, bi_ref, bo_ref, eig_ref,
    out_ref,
    g_buf, a_buf, gq_buf, aq_buf, rg_buf, rgq_buf, bo, bi, eig, inv,
    g_acc, a_acc, gq_part, gq_recv, aq_part, aq_recv, aq_mask, x_acc, norm_acc, msg, sums,
    ring_send, ring_recv, x_send, x_recv, xg_send, xg_recv, z_send, z_recv, local_sem,
):
    half = nz // 2
    stages = half // 2
    me = lax.axis_index("block")
    dp = lax.axis_index("dp")
    n_in, n_t = a_ref.shape
    n_out = g_ref.shape[0]
    n_c = aq_ref.shape[1]
    q_in, q_out = n_in // nx, n_out // nx
    per_dp = nz // nx
    my_rows = pl.ds(pl.multiple_of(dp * q_out, q_out), q_out)

    def z_peer(k):
        return {"block": lax.rem(me + (k + nz), nz)}

    def x_peer(k):
        return {"dp": lax.rem(dp + k, nx)}

    def source(slot):
        return lax.rem(me + nz - slot, nz)

    locals_ = [
        pltpu.make_async_copy(gq_ref.at[my_rows], gq_buf.at[0], local_sem.at[0]),
        pltpu.make_async_copy(aq_ref.at[pl.ds(pl.multiple_of(dp * q_in, q_in), q_in)], aq_buf.at[0], local_sem.at[1]),
        pltpu.make_async_copy(eig_ref, eig, local_sem.at[2]),
        pltpu.make_async_copy(g_ref, g_buf.at[0], local_sem.at[3]),
        pltpu.make_async_copy(bo_ref, bo, local_sem.at[4]),
        pltpu.make_async_copy(a_ref, a_buf.at[0], local_sem.at[5]),
        pltpu.make_async_copy(bi_ref, bi, local_sem.at[6]),
    ]
    for copy in locals_:
        copy.start()

    barrier = pltpu.get_barrier_semaphore()
    near = (1, 2, -1, -2)
    for k in near:
        pl.semaphore_signal(barrier, inc=1, device_id=z_peer(k), device_id_type=MESH)
    for k in range(1, nx):
        pl.semaphore_signal(barrier, inc=1, device_id=x_peer(k), device_id_type=MESH)

    def remote(src, dst, send_sem, recv_sem, device):
        return pltpu.make_async_remote_copy(
            src_ref=src, dst_ref=dst, send_sem=send_sem, recv_sem=recv_sem,
            device_id=device, device_id_type=MESH,
        )

    def extent(way, part, lo, size):
        if not part:
            return pl.ds(lo, size)
        return pl.ds(lo + way * (size // 2), size // 2)

    class Ring:
        def __init__(self, index, buf, first, lo, size):
            self.index, self.buf, self.first, self.lo, self.size = index, buf, first, lo, size

        def copy(self, way, hop, part, own=False):
            rows = extent(way, part, self.lo, self.size)
            src_slot, dst_slot = (hop, hop + 1) if way == 0 else (lax.rem(nz - hop, nz), nz - 1 - hop)
            src = self.first.at[rows] if own else self.buf.at[src_slot, rows]
            return remote(
                src, self.buf.at[dst_slot, rows], ring_send.at[self.index, way, hop],
                ring_recv.at[self.index, way, hop], z_peer(1 if way == 0 else -1),
            )

        def begin(self):
            for way in (0, 1):
                self.copy(way, 0, False, own=True).start()

        def relay(self, hop):
            for way in (0, 1):
                self.copy(way, hop - 1, False).wait_recv()
                self.copy(way, hop, False).start()

        def relay_last(self):
            for way in (0, 1):
                self.copy(way, half - 2, False).wait_recv()
                self.copy(way, half - 1, True).start()

        def end(self):
            for way in (0, 1):
                self.copy(way, half - 1, True).wait_recv()

        def at(self, hop):
            pl.when(hop < half - 1)(lambda: self.relay(hop))
            pl.when(hop == half - 1)(self.relay_last)
            pl.when(hop == half)(self.end)

        def sent(self):
            def body(hop, c):
                for way in (0, 1):
                    self.copy(way, hop, False).wait_send()
                return c

            lax.fori_loop(0, half - 1, body, 0)
            for way in (0, 1):
                self.copy(way, half - 1, True).wait_send()

    class Stride:
        def __init__(self, index, buf, lo, size):
            self.index, self.buf, self.lo, self.size = index, buf, lo, size

        def copy(self, way, stage, ahead, part=False):
            rows = extent(way, part, self.lo, self.size)
            base = 2 * (stage - 1)
            src_slot, dst_slot = (base, base + ahead) if way == 0 else (lax.rem(nz - base, nz), nz - base - ahead)
            sem = base + ahead - 1
            return remote(
                self.buf.at[src_slot, rows], self.buf.at[dst_slot, rows], ring_send.at[self.index, way, sem],
                ring_recv.at[self.index, way, sem], z_peer(ahead if way == 0 else -ahead),
            )

        def send(self, stage, last=False):
            for way in (0, 1):
                self.copy(way, stage, 2, last).start()
            for way in (0, 1):
                self.copy(way, stage, 1).start()

        def take(self, stage, last=False):
            for way in (0, 1):
                self.copy(way, stage, 2, last).wait_recv()
            for way in (0, 1):
                self.copy(way, stage, 1).wait_recv()

        def relay(self, stage, last):
            for way in (0, 1):
                self.copy(way, stage, 2).wait_recv()
                self.copy(way, stage + 1, 2, last).start()
                self.copy(way, stage + 1, 1).start()
            for way in (0, 1):
                self.copy(way, stage, 1).wait_recv()

        def sent(self):
            for stage in range(1, stages + 1):
                for way in (0, 1):
                    self.copy(way, stage, 2, stage == stages).wait_send()
                    self.copy(way, stage, 1).wait_send()

    ho = n_out // 2
    gq_ring = Stride(0, gq_buf, 0, q_out)
    aq_ring = Stride(1, aq_buf, 0, q_in)
    rgq_ring = Stride(2, rgq_buf, pl.multiple_of(dp * q_out, q_out), q_out)
    g_rings = (Ring(3, g_buf, g_ref, 0, ho), Ring(4, g_buf, g_ref, ho, ho))
    rg_rings = (Ring(5, rg_buf, rg_buf.at[0], 0, ho), Ring(6, rg_buf, rg_buf.at[0], ho, ho))
    a_ring = Ring(7, a_buf, a_ref, 0, n_in)

    locals_[0].wait()
    locals_[1].wait()
    pl.semaphore_wait(barrier, len(near) + nx - 1)

    gq_ring.send(1)
    for ring in g_rings:
        ring.begin()
    aq_ring.send(1)

    locals_[2].wait()
    for k in range(per_dp):
        inv[dp * per_dp + k] = 1.0 / (eig[:, k * n_out:(k + 1) * n_out] + DAMPING)

    def inv_copy(k, hop):
        owner = lax.rem(dp + nx - k * hop, nx)
        if hop == 0:
            rows = pl.ds(owner * per_dp, per_dp)
        else:
            rows = pl.ds(owner * per_dp + (0 if k == 1 else per_dp // 2), per_dp // 2)
        sem = 2 * hop + (0 if k == 1 else 1)
        return remote(inv.at[rows], inv.at[rows], x_send.at[0, sem], x_recv.at[0, sem], x_peer(lax.rem(k + nx, nx)))

    def inv_send(hop):
        for k in (1, -1):
            inv_copy(k, hop).start()

    def inv_take(hop):
        for k in (1, -1):
            owner = lax.rem(dp + nx - k * (hop + 1), nx)
            if hop == 0:
                rows = pl.ds(owner * per_dp, per_dp)
            else:
                rows = pl.ds(owner * per_dp + (0 if k == 1 else per_dp // 2), per_dp // 2)
            sem = 2 * hop + (0 if k == 1 else 1)
            remote(
                inv.at[rows], inv.at[rows], x_send.at[0, sem], x_recv.at[0, sem], x_peer(lax.rem(k + nx, nx))
            ).wait_recv()

    inv_send(0)

    def rotate_g(slot):
        rows = pl.ds(pl.multiple_of(source(slot) * n_out, n_out), n_out)
        return contract_rows(bo[rows, :], g_buf[slot])

    def rotate_a(slot):
        rows = pl.ds(pl.multiple_of(source(slot) * n_in, n_in), n_in)
        return contract_rows(bi[rows, :], a_buf[slot])

    for copy in locals_[3:]:
        copy.wait()
    g_acc[...] = rotate_g(0)
    a_acc[...] = rotate_a(0)
    x_acc[...] = jnp.zeros_like(x_acc)
    norm_acc[...] = jnp.zeros_like(norm_acc)

    def stack(ref, width, n):
        pieces = []
        for slot in range(nz):
            at = pl.multiple_of(source(slot) * width + dp * n, n)
            pieces.append(ref[pl.ds(at, n), :])
        return jnp.concatenate(pieces, axis=0)

    def gq_copy(k):
        rows = pl.ds(pl.multiple_of(lax.rem(dp + k, nx) * q_out, q_out), q_out)
        return remote(gq_part.at[rows], gq_recv.at[k - 1], x_send.at[1, k - 1], x_recv.at[1, k - 1], x_peer(k))

    def aq_copy(k):
        return remote(aq_part, aq_recv.at[k - 1], x_send.at[2, k - 1], x_recv.at[2, k - 1], x_peer(k))

    def query_sums():
        gq_ring.take(stages, True)
        gq_part[...] = contract_rows(stack(bo, n_out, q_out), gq_buf[...].reshape(nz * q_out, n_c))
        for k in range(1, nx):
            gq_copy(k).start()
        aq_ring.take(stages, True)
        aq_part[...] = contract_rows(stack(bi, n_in, q_in), aq_buf[...].reshape(nz * q_in, n_c))
        for k in range(1, nx):
            aq_copy(k).start()

    def rgq_copy(first, n, k, theirs=False):
        rows = pl.ds(pl.multiple_of(lax.rem(dp + nx - k, nx) * q_out, q_out), q_out) if theirs else my_rows
        ref = rgq_buf.at[pl.ds(first, n), rows]
        return remote(ref, ref, xg_send.at[first, k - 1], xg_recv.at[first, k - 1], x_peer(k))

    def gather_groups(stage):
        if isinstance(stage, int) and stage == 0:
            return ((0, 1),)
        if isinstance(stage, int) and stage == stages:
            return ((2 * stage - 1, 3),)
        return ((2 * stage - 1, 2), (nz - 2 * stage, 2))

    def gather(stage):
        for first, n in gather_groups(stage):
            for k in range(1, nx):
                rgq_copy(first, n, k).start()

    def gathered(stage):
        for first, n in gather_groups(stage):
            for k in range(1, nx):
                rgq_copy(first, n, k, theirs=True).wait_recv()

    def query_rotations():
        for k in range(1, nx):
            gq_copy(k).wait_recv()
        rgq_buf[0, my_rows] = (gq_part[my_rows] + gq_recv[0] + gq_recv[1] + gq_recv[2]).astype(BF16)
        rgq_ring.send(1)
        gather(0)
        for k in range(1, nx):
            aq_copy(k).wait_recv()
        rot_aq = (aq_part[...] + aq_recv[0] + aq_recv[1] + aq_recv[2]).astype(BF16).astype(F32)
        column = lax.broadcasted_iota(jnp.int32, (n_in, n_c), 1)
        for q in range(NQ):
            aq_mask[q * n_in:(q + 1) * n_in, :] = jnp.where(column // QSTEPS == q, rot_aq, 0.0).astype(BF16)

    def first_body(hop, c):
        @pl.when(hop < stages - 1)
        def _():
            gq_ring.relay(hop, False)

        @pl.when(hop == stages - 1)
        def _():
            gq_ring.relay(stages - 1, True)

        for ring in g_rings:
            ring.at(hop)

        @pl.when(hop < stages - 1)
        def _():
            aq_ring.relay(hop, False)

        @pl.when(hop == stages - 1)
        def _():
            aq_ring.relay(stages - 1, True)
            inv_take(0)
            inv_send(1)

        pl.when(hop == stages)(query_sums)
        pl.when(hop == stages + 1)(query_rotations)

        @pl.when(hop == stages + 2)
        def _():
            rgq_ring.relay(1, False)
            gather(1)

        @pl.when(hop == stages + 3)
        def _():
            rgq_ring.relay(2, False)
            gather(2)

        pl.when(hop == a_lead)(a_ring.begin)
        pl.when(hop > a_lead)(lambda: a_ring.relay(hop - a_lead))

        g_acc[...] += rotate_g(hop) + rotate_g(nz - hop)
        return c

    lax.fori_loop(1, half, first_body, 0)
    for ring in g_rings:
        ring.end()
    rg_buf[0] = (g_acc[...] + rotate_g(half)).astype(BF16)
    for ring in rg_rings:
        ring.begin()
    rgq_ring.relay(stages - 1, True)
    gather(stages - 1)
    a_ring.relay(half - a_lead)
    inv_take(1)
    gathered(0)

    group = 2

    def score_block(slot):
        block_inv = inv[source(slot)]
        queries = rgq_buf[slot]
        train = rg_buf[slot]
        for part in range(NQ // group):
            rows = pl.ds(part * group * n_in, group * n_in)
            grad = lax.dot_general(
                aq_mask[rows, :], queries, (((1,), (1,)), ((), ())), preferred_element_type=F32
            ).reshape(group, n_in, n_out)
            precond = grad * block_inv[None]
            terms = (grad * precond).reshape(group, n_in // 8, 8, n_out).sum(axis=1)
            for lane in range(n_out // 128):
                norm_acc[part * group:(part + 1) * group] += terms[:, :, lane * 128:(lane + 1) * 128]
            x_acc[rows, :] += jnp.dot(
                precond.astype(BF16).reshape(group * n_in, n_out), train, preferred_element_type=F32
            )

    def second_body(hop, c):
        for ring in rg_rings:
            ring.at(hop)

        @pl.when(hop == 1)
        def _():
            rgq_ring.take(stages, True)
            gather(stages)

        pl.when(hop + half - a_lead <= half)(lambda: a_ring.at(hop + half - a_lead))

        @pl.when(lax.rem(hop, 2) == 1)
        def _():
            stage = (hop + 1) // 2
            pl.when(stage < stages)(lambda: gathered(stage))
            pl.when(stage == stages)(lambda: gathered(stages))

        pl.when(hop == 1)(lambda: score_block(0))

        def blocks(i, c):
            slot = jnp.where(i == 0, hop, nz - hop)
            score_block(slot)
            a_acc[...] += rotate_a(slot)
            return c

        lax.fori_loop(0, jnp.where(hop == half, 1, 2), blocks, 0)
        return c

    lax.fori_loop(1, half + 1, second_body, 0)

    rot_a = a_acc[...].astype(BF16).astype(F32)
    for q in range(NQ):
        g_acc[q:q + 1, :] = jnp.sum(x_acc[q * n_in:(q + 1) * n_in, :] * rot_a, axis=0, keepdims=True)
    step_of = lax.broadcasted_iota(jnp.int32, (n_t, 128), 0) // STEPS
    episode = lax.broadcasted_iota(jnp.int32, (n_t, 128), 1)
    pick = jnp.where(step_of == episode, 1.0, 0.0)
    scores = jnp.dot(
        g_acc[0:NQ, :], pick, preferred_element_type=F32, precision=lax.Precision.HIGHEST
    )
    norms = jnp.sum(jnp.sum(norm_acc[...], axis=1), axis=1, keepdims=True)
    lanes = lax.broadcasted_iota(jnp.int32, (NQ, 128), 1)
    msg[...] = jnp.where(lanes == 127, norms, scores)

    def sum_copy(k):
        return remote(msg, sums.at[k - 1], z_send.at[k - 1], z_recv.at[k - 1], z_peer(k))

    order = sorted(range(1, nz), key=lambda k: -min(k, nz - k))
    for k in order:
        sum_copy(k).start()

    for ring in (gq_ring, aq_ring, rgq_ring) + g_rings + rg_rings + (a_ring,):
        ring.sent()
    for hop in (0, 1):
        for k in (1, -1):
            inv_copy(k, hop).wait_send()
    for k in range(1, nx):
        gq_copy(k).wait_send()
        aq_copy(k).wait_send()
    for stage in range(stages + 1):
        for start, n in gather_groups(stage):
            for k in range(1, nx):
                rgq_copy(start, n, k).wait_send()

    total = msg[...]
    for k in range(1, nz):
        sum_copy(k).wait_recv()
        total += sums[k - 1]
    out_ref[...] = (total / jnp.sqrt(total[:, 127:128] * QSTEPS))[:, : out_ref.shape[1]]
    for k in range(1, nz):
        sum_copy(k).wait_send()


def shards(nz, nx, a_train, g_train, a_query, g_query, basis_in, basis_out, eigen):
    n_in, n_t = a_train.shape
    n_out = g_train.shape[0]
    n_c = a_query.shape[1]
    q_in, q_out = n_in // nx, n_out // nx
    vmem = pltpu.VMEM
    dma = pltpu.SemaphoreType.DMA
    return pl.pallas_call(
        functools.partial(kernel, nz, nx, nz // 2 - 2),
        out_shape=jax.ShapeDtypeStruct((NQ, n_t // STEPS), F32),
        in_specs=[pl.BlockSpec(memory_space=pl.ANY)] * 7,
        out_specs=pl.BlockSpec(memory_space=vmem),
        scratch_shapes=[
            vmem((nz, n_out, n_t), BF16),
            vmem((nz, n_in, n_t), BF16),
            vmem((nz, q_out, n_c), BF16),
            vmem((nz, q_in, n_c), BF16),
            vmem((nz, n_out, n_t), BF16),
            vmem((nz, n_out, n_c), BF16),
            vmem(basis_out.shape, BF16),
            vmem(basis_in.shape, BF16),
            vmem(eigen.shape, F32),
            vmem((nz, n_in, n_out), F32),
            vmem((n_out, n_t), F32),
            vmem((n_in, n_t), F32),
            vmem((n_out, n_c), F32),
            vmem((nx - 1, q_out, n_c), F32),
            vmem((n_in, n_c), F32),
            vmem((nx - 1, n_in, n_c), F32),
            vmem((NQ * n_in, n_c), BF16),
            vmem((NQ * n_in, n_t), F32),
            vmem((NQ, 8, 128), F32),
            vmem((NQ, 128), F32),
            vmem((nz - 1, NQ, 128), F32),
            dma((8, 2, nz // 2)),
            dma((8, 2, nz // 2)),
            dma((3, 4)),
            dma((3, 4)),
            dma((nz, nx - 1)),
            dma((nz, nx - 1)),
            dma((nz - 1,)),
            dma((nz - 1,)),
            dma((7,)),
        ],
        compiler_params=pltpu.CompilerParams(
            collective_id=0, has_side_effects=True, vmem_limit_bytes=56 * 2**20
        ),
    )(a_train, g_train, a_query, g_query, basis_in, basis_out, eigen)


def solution(mesh):
    in_specs = (
        P(("member", "block"), "dp"),
        P(("member", "block"), "dp"),
        P(("member", "block"), None),
        P(("member", "block"), None),
        P("member", "block"),
        P("member", "block"),
        P(("member", "block"), "dp"),
    )
    body = functools.partial(shards, mesh.shape["block"], mesh.shape["dp"])
    return jax.shard_map(body, mesh=mesh, in_specs=in_specs, out_specs=P("member", "dp"), check_vma=False)
```

time: 435 us -> 98.1 us (0.23)
  waiting for transfers between devices: 232 us -> 0 us
  blocking collectives: 169 us -> 0 us
  Pallas kernels: 0 us -> 96.5 us
  matrix products: 14.4 us -> 0 us
  between operations: 13.2 us -> 0.01 us
    all_gather x4 -> x0, waiting for transfers between devices: 232 us -> none  [the longest x1 84.1 us: shards(): rot_g = lax.all_gather(rot_g_local, 'block', axis=0, tiled=True)]
    psum x2 -> x0, blocking collectives: 169 us -> none  [the longest x1 142 us: shards(): norm_value = lax.psum(norm_terms, ('dp', 'block'))]
    pallas_call x0 -> x1, Pallas kernels: none -> 96.5 us  [shards(): pl.pallas_call(functools.partial(kernel, nz, nx, nz // 2 - 2), out_shape=...]
    dot_general x4 -> x0, matrix products: 14.4 us -> none  [the longest x1 6.36 us: score_terms(): jnp.einsum('qij,jr->qir', precond, rot_gt, preferred_element_type=jnp.flo...]
  transfers between devices with their start and end apart: 4 -> 0, of which waited for: 3 -> 0; matrix products, arithmetic and copies ran while one was open for 2% -> 0% of each run, Pallas kernels for 0% -> 0%
where the time goes in v2:
time: 98.1 us; the launch traced here: 97.8 us
  Pallas kernels  96.5 us (98%)
  local copies, waits for them, and re-layouts  1.28 us (1%)
    pallas_call x1, Pallas kernels, shards(): pl.pallas_call(functools.partial(kernel, nz, nx, nz // 2 - 2), out_shape=...  96.5 us

profile of v2, /device:TPU:24, one launch (start us, length us, event | category | flops | bytes accessed | tf_op | source)
XLA Modules:
  0.0 97.8 jit_solution(7677552312050971491)
XLA Ops:
  0.0 96.5 %shard_map.73 = f32[8,16]{1,0:T(8,128)} custom-call(bf16[128,256]{1,0:T(8,128)(2,1)} %a_ref.1, bf16[256,256]{1,0:T(8,128)(2,1)} %g_ref.1, bf16[128,128]{1,0:T(8,128)(2,1)} %aq_ref.1, bf16[256,128]{1,0:T(8,128)(2,1)} %gq_ref.1, bf16[2048,128]{1,0:T(8,128)(2,1)} %bi_ref.1, bf16[4096,256]{1,0:T(8,128)(2,1)} %bo_ref.1, f32[128,1024]{1,0:T(8,128)} %eig_ref.1), custom_call_target="tpu_custom_call" | custom-call | tf_op jit(solution)/shard_map/pallas_call | solution.py:441
  96.6 1.3 %copy.9 = f32[8,16]{1,0:T(8,128)} copy(f32[8,16]{1,0:T(8,128)} %shard_map.73) | data formatting | bytes 1024

commit v3 on v2

--- a/solution.py
+++ b/solution.py
@@ -12,6 +12,12 @@
 QSTEPS = 16
 DAMPING = 0.05
 
+A_LEAD = 6
+Q_SUM = 4
+Q_ROT = 6
+G_CUTS = 4
+A_CUTS = 2
+
 MESH = pl.DeviceIdType.MESH
 BF16 = jnp.bfloat16
 F32 = jnp.float32
@@ -22,7 +28,7 @@
 
 
 def kernel(
-    nz, nx, a_lead,
+    nz, nx, g_cuts, a_cuts,
     a_ref, g_ref, aq_ref, gq_ref, bi_ref, bo_ref, eig_ref,
     out_ref,
     g_buf, a_buf, gq_buf, aq_buf, rg_buf, rgq_buf, bo, bi, eig, inv,
@@ -165,13 +171,13 @@
                     self.copy(way, stage, 2, stage == stages).wait_send()
                     self.copy(way, stage, 1).wait_send()
 
-    ho = n_out // 2
+    ho, hi = n_out // g_cuts, n_in // a_cuts
     gq_ring = Stride(0, gq_buf, 0, q_out)
-    aq_ring = Stride(1, aq_buf, 0, q_in)
-    rgq_ring = Stride(2, rgq_buf, pl.multiple_of(dp * q_out, q_out), q_out)
-    g_rings = (Ring(3, g_buf, g_ref, 0, ho), Ring(4, g_buf, g_ref, ho, ho))
-    rg_rings = (Ring(5, rg_buf, rg_buf.at[0], 0, ho), Ring(6, rg_buf, rg_buf.at[0], ho, ho))
-    a_ring = Ring(7, a_buf, a_ref, 0, n_in)
+    aq_ring = Ring(1, aq_buf, aq_buf.at[0], 0, q_in)
+    rgq_ring = Ring(2, rgq_buf, rgq_buf.at[0], pl.multiple_of(dp * q_out, q_out), q_out)
+    g_rings = tuple(Ring(3 + c, g_buf, g_ref, c * ho, ho) for c in range(g_cuts))
+    rg_rings = tuple(Ring(3 + g_cuts + c, rg_buf, rg_buf.at[0], c * ho, ho) for c in range(g_cuts))
+    a_rings = tuple(Ring(3 + 2 * g_cuts + c, a_buf, a_ref, c * hi, hi) for c in range(a_cuts))
 
     locals_[0].wait()
     locals_[1].wait()
@@ -180,7 +186,7 @@
     gq_ring.send(1)
     for ring in g_rings:
         ring.begin()
-    aq_ring.send(1)
+    aq_ring.begin()
 
     locals_[2].wait()
     for k in range(per_dp):
@@ -247,39 +253,34 @@
         gq_part[...] = contract_rows(stack(bo, n_out, q_out), gq_buf[...].reshape(nz * q_out, n_c))
         for k in range(1, nx):
             gq_copy(k).start()
-        aq_ring.take(stages, True)
+
+    def query_sums_in():
+        aq_ring.end()
         aq_part[...] = contract_rows(stack(bi, n_in, q_in), aq_buf[...].reshape(nz * q_in, n_c))
         for k in range(1, nx):
             aq_copy(k).start()
 
-    def rgq_copy(first, n, k, theirs=False):
+    def rgq_copy(slot, k, theirs=False):
         rows = pl.ds(pl.multiple_of(lax.rem(dp + nx - k, nx) * q_out, q_out), q_out) if theirs else my_rows
-        ref = rgq_buf.at[pl.ds(first, n), rows]
-        return remote(ref, ref, xg_send.at[first, k - 1], xg_recv.at[first, k - 1], x_peer(k))
-
-    def gather_groups(stage):
-        if isinstance(stage, int) and stage == 0:
-            return ((0, 1),)
-        if isinstance(stage, int) and stage == stages:
-            return ((2 * stage - 1, 3),)
-        return ((2 * stage - 1, 2), (nz - 2 * stage, 2))
-
-    def gather(stage):
-        for first, n in gather_groups(stage):
-            for k in range(1, nx):
-                rgq_copy(first, n, k).start()
-
-    def gathered(stage):
-        for first, n in gather_groups(stage):
-            for k in range(1, nx):
-                rgq_copy(first, n, k, theirs=True).wait_recv()
+        ref = rgq_buf.at[slot, rows]
+        return remote(ref, ref, xg_send.at[slot, k - 1], xg_recv.at[slot, k - 1], x_peer(k))
+
+    def gather(slot):
+        for k in range(1, nx):
+            rgq_copy(slot, k).start()
+
+    def gathered(slot):
+        for k in range(1, nx):
+            rgq_copy(slot, k, theirs=True).wait_recv()
 
     def query_rotations():
         for k in range(1, nx):
             gq_copy(k).wait_recv()
         rgq_buf[0, my_rows] = (gq_part[my_rows] + gq_recv[0] + gq_recv[1] + gq_recv[2]).astype(BF16)
-        rgq_ring.send(1)
+        rgq_ring.begin()
         gather(0)
+
+    def query_rotations_in():
         for k in range(1, nx):
             aq_copy(k).wait_recv()
         rot_aq = (aq_part[...] + aq_recv[0] + aq_recv[1] + aq_recv[2]).astype(BF16).astype(F32)
@@ -299,46 +300,43 @@
         for ring in g_rings:
             ring.at(hop)
 
-        @pl.when(hop < stages - 1)
-        def _():
-            aq_ring.relay(hop, False)
+        aq_ring.at(hop)
 
         @pl.when(hop == stages - 1)
         def _():
-            aq_ring.relay(stages - 1, True)
             inv_take(0)
             inv_send(1)
 
-        pl.when(hop == stages)(query_sums)
-        pl.when(hop == stages + 1)(query_rotations)
-
-        @pl.when(hop == stages + 2)
-        def _():
-            rgq_ring.relay(1, False)
-            gather(1)
-
-        @pl.when(hop == stages + 3)
-        def _():
-            rgq_ring.relay(2, False)
-            gather(2)
-
-        pl.when(hop == a_lead)(a_ring.begin)
-        pl.when(hop > a_lead)(lambda: a_ring.relay(hop - a_lead))
+        pl.when(hop == Q_SUM)(query_sums)
+        pl.when(hop == Q_ROT)(query_rotations)
+
+        @pl.when(hop > Q_ROT)
+        def _():
+            rgq_ring.relay(hop - Q_ROT)
+            gather(hop - Q_ROT)
+            gather(nz - hop + Q_ROT)
+
+        pl.when(hop == A_LEAD)(a_rings[0].begin)
+        pl.when(hop > A_LEAD)(lambda: a_rings[0].relay(hop - A_LEAD))
 
         g_acc[...] += rotate_g(hop) + rotate_g(nz - hop)
         return c
 
     lax.fori_loop(1, half, first_body, 0)
+    for ring in a_rings[1:]:
+        ring.begin()
     for ring in g_rings:
         ring.end()
     rg_buf[0] = (g_acc[...] + rotate_g(half)).astype(BF16)
     for ring in rg_rings:
         ring.begin()
-    rgq_ring.relay(stages - 1, True)
-    gather(stages - 1)
-    a_ring.relay(half - a_lead)
+    a_rings[0].relay(half - A_LEAD)
+    early = half - Q_ROT
+    rgq_ring.relay(early)
+    gather(early)
+    gather(nz - early)
+    query_sums_in()
     inv_take(1)
-    gathered(0)
 
     group = 2
 
@@ -363,28 +361,48 @@
         for ring in rg_rings:
             ring.at(hop)
 
-        @pl.when(hop == 1)
-        def _():
-            rgq_ring.take(stages, True)
-            gather(stages)
-
-        pl.when(hop + half - a_lead <= half)(lambda: a_ring.at(hop + half - a_lead))
-
-        @pl.when(lax.rem(hop, 2) == 1)
-        def _():
-            stage = (hop + 1) // 2
-            pl.when(stage < stages)(lambda: gathered(stage))
-            pl.when(stage == stages)(lambda: gathered(stages))
-
-        pl.when(hop == 1)(lambda: score_block(0))
+        pl.when(hop <= A_LEAD)(lambda: a_rings[0].at(hop + half - A_LEAD))
+        for ring in a_rings[1:]:
+            ring.at(hop)
+
+        @pl.when(hop <= Q_ROT)
+        def _():
+            rgq_ring.at(hop + early)
+
+        @pl.when(hop < Q_ROT)
+        def _():
+            gather(hop + early)
+            gather(nz - hop - early)
+
+        pl.when(hop == Q_ROT)(lambda: gather(half))
+
+        @pl.when(hop == 2)
+        def _():
+            query_rotations_in()
+            for slot in (0, 1, nz - 1):
+                gathered(slot)
+            score_block(0)
+
+        @pl.when((hop > 1) & (hop < half))
+        def _():
+            gathered(hop)
+            gathered(nz - hop)
+
+        pl.when(hop == half)(lambda: gathered(half))
 
         def blocks(i, c):
+            slot = jnp.where(i == 0, hop, jnp.where(i == 1, nz - hop, jnp.where(i == 2, 1, nz - 1)))
+            score_block(slot)
+            return c
+
+        lax.fori_loop(0, jnp.where(hop == 1, 0, jnp.where(hop == half, 1, jnp.where(hop == 2, 4, 2))), blocks, 0)
+
+        def inputs(i, c):
             slot = jnp.where(i == 0, hop, nz - hop)
-            score_block(slot)
             a_acc[...] += rotate_a(slot)
             return c
 
-        lax.fori_loop(0, jnp.where(hop == half, 1, 2), blocks, 0)
+        lax.fori_loop(0, jnp.where(hop == half, 1, 2), inputs, 0)
         return c
 
     lax.fori_loop(1, half + 1, second_body, 0)
@@ -392,15 +410,18 @@
     rot_a = a_acc[...].astype(BF16).astype(F32)
     for q in range(NQ):
         g_acc[q:q + 1, :] = jnp.sum(x_acc[q * n_in:(q + 1) * n_in, :] * rot_a, axis=0, keepdims=True)
+    n_e = n_t // STEPS
     step_of = lax.broadcasted_iota(jnp.int32, (n_t, 128), 0) // STEPS
-    episode = lax.broadcasted_iota(jnp.int32, (n_t, 128), 1)
-    pick = jnp.where(step_of == episode, 1.0, 0.0)
+    lane = lax.broadcasted_iota(jnp.int32, (n_t, 128), 1)
+    pick = jnp.where(step_of == lane % n_e, 1.0, 0.0)
     scores = jnp.dot(
         g_acc[0:NQ, :], pick, preferred_element_type=F32, precision=lax.Precision.HIGHEST
     )
     norms = jnp.sum(jnp.sum(norm_acc[...], axis=1), axis=1, keepdims=True)
-    lanes = lax.broadcasted_iota(jnp.int32, (NQ, 128), 1)
-    msg[...] = jnp.where(lanes == 127, norms, scores)
+    query = lax.broadcasted_iota(jnp.int32, (NQ, 128), 0)
+    mine = lax.broadcasted_iota(jnp.int32, (NQ, 128), 1) // n_e == query
+    msg[0:1, :] = jnp.sum(jnp.where(mine, scores, 0.0), axis=0, keepdims=True)
+    msg[1:2, :] = jnp.sum(jnp.where(mine, norms, 0.0), axis=0, keepdims=True)
 
     def sum_copy(k):
         return remote(msg, sums.at[k - 1], z_send.at[k - 1], z_recv.at[k - 1], z_peer(k))
@@ -409,7 +430,7 @@
     for k in order:
         sum_copy(k).start()
 
-    for ring in (gq_ring, aq_ring, rgq_ring) + g_rings + rg_rings + (a_ring,):
+    for ring in (gq_ring, aq_ring, rgq_ring) + g_rings + rg_rings + a_rings:
         ring.sent()
     for hop in (0, 1):
         for k in (1, -1):
@@ -417,16 +438,18 @@
     for k in range(1, nx):
         gq_copy(k).wait_send()
         aq_copy(k).wait_send()
-    for stage in range(stages + 1):
-        for start, n in gather_groups(stage):
-            for k in range(1, nx):
-                rgq_copy(start, n, k).wait_send()
-
+
+    def sent_body(slot, c):
+        for k in range(1, nx):
+            rgq_copy(slot, k).wait_send()
+        return c
+
+    lax.fori_loop(0, nz, sent_body, 0)
     total = msg[...]
     for k in range(1, nz):
         sum_copy(k).wait_recv()
         total += sums[k - 1]
-    out_ref[...] = (total / jnp.sqrt(total[:, 127:128] * QSTEPS))[:, : out_ref.shape[1]]
+    out_ref[...] = total[0:1, :] / jnp.sqrt(total[1:2, :] * QSTEPS)
     for k in range(1, nz):
         sum_copy(k).wait_send()
 
@@ -438,9 +461,9 @@
     q_in, q_out = n_in // nx, n_out // nx
     vmem = pltpu.VMEM
     dma = pltpu.SemaphoreType.DMA
-    return pl.pallas_call(
-        functools.partial(kernel, nz, nx, nz // 2 - 2),
-        out_shape=jax.ShapeDtypeStruct((NQ, n_t // STEPS), F32),
+    total = pl.pallas_call(
+        functools.partial(kernel, nz, nx, G_CUTS, A_CUTS),
+        out_shape=jax.ShapeDtypeStruct((1, 128), F32),
         in_specs=[pl.BlockSpec(memory_space=pl.ANY)] * 7,
         out_specs=pl.BlockSpec(memory_space=vmem),
         scratch_shapes=[
@@ -463,10 +486,10 @@
             vmem((NQ * n_in, n_c), BF16),
             vmem((NQ * n_in, n_t), F32),
             vmem((NQ, 8, 128), F32),
-            vmem((NQ, 128), F32),
-            vmem((nz - 1, NQ, 128), F32),
-            dma((8, 2, nz // 2)),
-            dma((8, 2, nz // 2)),
+            vmem((2, 128), F32),
+            vmem((nz - 1, 2, 128), F32),
+            dma((3 + 2 * G_CUTS + A_CUTS, 2, nz // 2)),
+            dma((3 + 2 * G_CUTS + A_CUTS, 2, nz // 2)),
             dma((3, 4)),
             dma((3, 4)),
             dma((nz, nx - 1)),
@@ -479,6 +502,7 @@
             collective_id=0, has_side_effects=True, vmem_limit_bytes=56 * 2**20
         ),
     )(a_train, g_train, a_query, g_query, basis_in, basis_out, eigen)
+    return total.reshape(NQ, n_t // STEPS)
 
 
 def solution(mesh):

time: 98.1 us -> 95.7 us (0.976)
  Pallas kernels: 96.5 us -> 93 us
  other arithmetic: 0 us -> 1.34 us
    pallas_call x1, Pallas kernels: 96.5 us -> 93 us  [shards(): pl.pallas_call(functools.partial(kernel, nz, nx, G_CUTS, A_CUTS), out_sha...]
    pallas_call x0 -> x1, other arithmetic: none -> 1.34 us  [shards(): pl.pallas_call(functools.partial(kernel, nz, nx, G_CUTS, A_CUTS), out_sha...]
    unnamed x1 -> x0, local copies, waits for them, and re-layouts: 1.28 us -> none
where the time goes in v3:
time: 95.7 us; the launch traced here: 95.5 us
  Pallas kernels  93 us (97%)
  other arithmetic  1.34 us (1%)
  local copies, waits for them, and re-layouts  1.19 us (1%)
    pallas_call x1, Pallas kernels, shards(): pl.pallas_call(functools.partial(kernel, nz, nx, G_CUTS, A_CUTS), out_sha...  93 us

profile of v3, /device:TPU:24, one launch (start us, length us, event | category | flops | bytes accessed | tf_op | source)
XLA Modules:
  0.0 95.5 jit_solution(1391672171268732689)
XLA Ops:
  0.0 93.0 %shard_map.73 = f32[1,128]{1,0:T(1,128)} custom-call(bf16[128,256]{1,0:T(8,128)(2,1)} %a_ref.1, bf16[256,256]{1,0:T(8,128)(2,1)} %g_ref.1, bf16[128,128]{1,0:T(8,128)(2,1)} %aq_ref.1, bf16[256,128]{1,0:T(8,128)(2,1)} %gq_ref.1, bf16[2048,128]{1,0:T(8,128)(2,1)} %bi_ref.1, bf16[4096,256]{1,0:T(8,128)(2,1)} %bo_ref.1, f32[128,1024]{1,0:T(8,128)} %eig_ref.1), custom_call_target="tpu_custom_call" | custom-call | tf_op jit(solution)/shard_map/pallas_call | solution.py:464
  93.0 0.5 broadcast.3
  93.5 1.3 %reduce.3 = f32[128]{0:T(128)S(1)} reduce(f32[1,128]{1,0:T(1,128)} %shard_map.73, f32[]{:T(128)} %broadcast.3), dimensions={0}, to_apply=%pallas_call.3.reduce_sub_computation.3 | reduce | bytes 1028 | tf_op jit(solution)/shard_map/pallas_call | solution.py:464
  94.8 0.7 reshape.3

commit v4 on v3

--- a/solution.py
+++ b/solution.py
@@ -12,11 +12,11 @@
 QSTEPS = 16
 DAMPING = 0.05
 
-A_LEAD = 6
+A_LEADS = (5, 7)
 Q_SUM = 4
 Q_ROT = 6
 G_CUTS = 4
-A_CUTS = 2
+A_CUTS = len(A_LEADS)
 
 MESH = pl.DeviceIdType.MESH
 BF16 = jnp.bfloat16
@@ -316,21 +316,21 @@
             gather(hop - Q_ROT)
             gather(nz - hop + Q_ROT)
 
-        pl.when(hop == A_LEAD)(a_rings[0].begin)
-        pl.when(hop > A_LEAD)(lambda: a_rings[0].relay(hop - A_LEAD))
+        for lead, ring in zip(A_LEADS, a_rings):
+            pl.when(hop == lead)(ring.begin)
+            pl.when(hop > lead)(functools.partial(lambda one, by: one.relay(hop - by), ring, lead))
 
         g_acc[...] += rotate_g(hop) + rotate_g(nz - hop)
         return c
 
     lax.fori_loop(1, half, first_body, 0)
-    for ring in a_rings[1:]:
-        ring.begin()
     for ring in g_rings:
         ring.end()
     rg_buf[0] = (g_acc[...] + rotate_g(half)).astype(BF16)
     for ring in rg_rings:
         ring.begin()
-    a_rings[0].relay(half - A_LEAD)
+    for lead, ring in zip(A_LEADS, a_rings):
+        ring.at(half - lead)
     early = half - Q_ROT
     rgq_ring.relay(early)
     gather(early)
@@ -358,12 +358,18 @@
             )
 
     def second_body(hop, c):
+        def inputs(i, c):
+            slot = jnp.where(i == 0, hop, nz - hop)
+            a_acc[...] += rotate_a(slot)
+            return c
+
+        lax.fori_loop(0, jnp.where(hop == half, 1, 2), inputs, 0)
+
         for ring in rg_rings:
             ring.at(hop)
 
-        pl.when(hop <= A_LEAD)(lambda: a_rings[0].at(hop + half - A_LEAD))
-        for ring in a_rings[1:]:
-            ring.at(hop)
+        for lead, ring in zip(A_LEADS, a_rings):
+            pl.when(hop <= lead)(functools.partial(lambda one, by: one.at(hop + half - by), ring, lead))
 
         @pl.when(hop <= Q_ROT)
         def _():
@@ -397,12 +403,6 @@
 
         lax.fori_loop(0, jnp.where(hop == 1, 0, jnp.where(hop == half, 1, jnp.where(hop == 2, 4, 2))), blocks, 0)
 
-        def inputs(i, c):
-            slot = jnp.where(i == 0, hop, nz - hop)
-            a_acc[...] += rotate_a(slot)
-            return c
-
-        lax.fori_loop(0, jnp.where(hop == half, 1, 2), inputs, 0)
         return c
 
     lax.fori_loop(1, half + 1, second_body, 0)

time: 95.7 us -> 95.4 us (level)
  no operation moved by 1% of the time
where the time goes in v4:
time: 95.4 us; the launch traced here: 95.2 us
  Pallas kernels  92.6 us (97%)
  other arithmetic  1.34 us (1%)
  local copies, waits for them, and re-layouts  1.19 us (1%)
    pallas_call x1, Pallas kernels, shards(): pl.pallas_call(functools.partial(kernel, nz, nx, G_CUTS, A_CUTS), out_sha...  92.6 us

profile of v4, /device:TPU:24, one launch (start us, length us, event | category | flops | bytes accessed | tf_op | source)
XLA Modules:
  0.0 95.2 jit_solution(6459684118423486784)
XLA Ops:
  0.0 92.6 %shard_map.73 = f32[1,128]{1,0:T(1,128)} custom-call(bf16[128,256]{1,0:T(8,128)(2,1)} %a_ref.1, bf16[256,256]{1,0:T(8,128)(2,1)} %g_ref.1, bf16[128,128]{1,0:T(8,128)(2,1)} %aq_ref.1, bf16[256,128]{1,0:T(8,128)(2,1)} %gq_ref.1, bf16[2048,128]{1,0:T(8,128)(2,1)} %bi_ref.1, bf16[4096,256]{1,0:T(8,128)(2,1)} %bo_ref.1, f32[128,1024]{1,0:T(8,128)} %eig_ref.1), custom_call_target="tpu_custom_call" | custom-call | tf_op jit(solution)/shard_map/pallas_call | solution.py:464
  92.6 0.5 broadcast.3
  93.2 1.3 %reduce.3 = f32[128]{0:T(128)S(1)} reduce(f32[1,128]{1,0:T(1,128)} %shard_map.73, f32[]{:T(128)} %broadcast.3), dimensions={0}, to_apply=%pallas_call.3.reduce_sub_computation.3 | reduce | bytes 1028 | tf_op jit(solution)/shard_map/pallas_call | solution.py:464
  94.5 0.7 reshape.3
